TPU v7x, 32 devices: a whole 2x2x4 slice. The times are simulated.
32 devices in a mesh: space: 8 (over z, x), tm: 4 (over y, core).
Axes of the slice: x: 2, y: 2, z: 4, core: 2. Of those that a mesh axis runs over, the one named last changes fastest.
Arguments:
- frame_slab: float32 [16384, 2048], P('space', 'tm'), may hold values from -160 to 160
- pair_decay_rates: float32 [32], replicated, may hold values from -2 to 0.5
- pair_angular_frequencies: float32 [32], replicated, as said below
Outputs:
- spatial_modes: float32 [64, 16384], P(None, 'space')
- misfit_matrix: float32 [16384, 2048], P('space', 'tm')
- gradient: float32 [64], replicated
- gauss_newton: float32 [64, 64], replicated
Inputs may be any that keep to these rules, and one draw needn't show every extreme that they name: pair_angular_frequencies[k] lies within 0.5 of 2 pi (k + 1).
All inputs are finite; a program needn't handle non-finite values.
Results may differ from a plain program's by a relative error of at most 0.0003.
Values sent between devices are 32-bit elements; how exact they have to be, the bound alone decides.
A program may use at most 64 MiB of HBM per device.

v0:
```python
import jax
import jax.numpy as jnp
from jax import lax
from jax.sharding import PartitionSpec as P

highest = lax.Precision.HIGHEST


def build_epoch_vectors(pair_decay_rates, pair_angular_frequencies, measured_epochs):
    shrinking_exponential = jnp.exp(pair_decay_rates[:, None] * measured_epochs[None, :])
    turning_radians = pair_angular_frequencies[:, None] * measured_epochs[None, :]
    joined_vectors = jnp.stack(
        [
            shrinking_exponential * jnp.cos(turning_radians),
            shrinking_exponential * jnp.sin(turning_radians),
        ],
        axis=1,
    )
    return joined_vectors.reshape(2 * pair_decay_rates.shape[0], measured_epochs.shape[0])


def coupling_table():
    return jnp.array([[[1.0, 0.0], [0.0, 1.0]], [[0.0, -1.0], [1.0, 0.0]]], dtype=jnp.float32)


def newton_terms(cross_term, mode_gram, slope_gram, magnitude_divisor):
    pairs = cross_term.shape[0] // 2
    coupling = coupling_table()
    cross_blocks = cross_term.reshape(pairs, 2, pairs, 2)
    indices = jnp.arange(pairs, dtype=jnp.int32)
    diagonal_blocks = cross_blocks[indices, :, indices, :]
    gradient = -magnitude_divisor * jnp.einsum(
        "puw,kuw->kp", coupling, diagonal_blocks, precision=highest
    )
    mode_blocks = mode_gram.reshape(pairs, 2, pairs, 2)
    slope_blocks = slope_gram.reshape(pairs, 2, pairs, 2)
    inner = jnp.einsum("kulv,kwlx->kuwlvx", mode_blocks, slope_blocks, precision=highest)
    gauss_newton = magnitude_divisor * jnp.einsum(
        "puw,kuwlvx,qvx->kplq", coupling, inner, coupling, precision=highest
    )
    return (gradient.reshape(2 * pairs), gauss_newton.reshape(2 * pairs, 2 * pairs))


def outer_sum(left, right):
    return jnp.dot(left, right.T, precision=highest, preferred_element_type=jnp.float32)


def local(frame_slab, pair_decay_rates, pair_angular_frequencies):
    point_count, epoch_number = frame_slab.shape
    epoch_partitions = lax.axis_size("tm")
    complete_epochs = epoch_number * epoch_partitions
    location_number = point_count * lax.axis_size("space")
    leading_shift = lax.axis_index("tm") * epoch_number
    every_instant = jnp.arange(complete_epochs, dtype=jnp.float32) / complete_epochs
    complete_basis = build_epoch_vectors(pair_decay_rates, pair_angular_frequencies, every_instant)
    complete_slope = complete_basis * every_instant[None, :]
    basis_gram = outer_sum(complete_basis, complete_basis)
    slope_gram = outer_sum(complete_slope, complete_slope)
    epoch_vector_set = lax.dynamic_slice_in_dim(complete_basis, leading_shift, epoch_number, 1)
    jacobian_lines = lax.dynamic_slice_in_dim(complete_slope, leading_shift, epoch_number, 1)
    projection_part = lax.dot_general(
        epoch_vector_set,
        frame_slab,
        (((1,), (1,)), ((), ())),
        precision=highest,
        preferred_element_type=jnp.float32,
    )
    factor = jnp.linalg.cholesky(basis_gram)
    projection = lax.psum(projection_part, "tm")
    spatial_modes = jax.scipy.linalg.cho_solve((factor, True), projection)
    fitted = lax.dot_general(
        spatial_modes,
        epoch_vector_set,
        (((0,), (0,)), ((), ())),
        precision=highest,
        preferred_element_type=jnp.float32,
    )
    misfit_matrix = frame_slab - fitted
    moment = lax.dot_general(
        misfit_matrix,
        jacobian_lines,
        (((1,), (1,)), ((), ())),
        precision=highest,
        preferred_element_type=jnp.float32,
    )
    cross_part = jnp.dot(
        spatial_modes, moment, precision=highest, preferred_element_type=jnp.float32
    )
    cross_term = lax.psum(cross_part, ("space", "tm"))
    mode_gram = lax.psum(outer_sum(spatial_modes, spatial_modes), "space")
    magnitude_divisor = 1.0 / (location_number * complete_epochs)
    gradient, gauss_newton = newton_terms(cross_term, mode_gram, slope_gram, magnitude_divisor)
    return (spatial_modes, misfit_matrix, gradient, gauss_newton)


def solution(mesh):
    placed = (P("space", "tm"), P(), P())
    return jax.shard_map(
        local,
        mesh=mesh,
        in_specs=placed,
        out_specs=(P(None, "space"), P("space", "tm"), P(), P()),
        check_vma=False,
    )
```

profile of v0, /device:TPU:0, one launch (start us, length us, event | category | flops | bytes accessed | tf_op | source)
XLA Modules:
  0.0 205.3 jit_solution(8120716566495042671)
XLA Ops:
  7.2 0.0 all-reduce.2.cloned.1.call-start
  7.2 1.7 fusion.6
  9.0 0.4 copy.37
  9.4 0.4 reshape.216
  9.8 7.0 %fusion.15 = f32[64,2048]{1,0:T(8,128)} fusion(f32[2048,512]{1,0:T(8,128)} %param.4, f32[64,2048]{1,0:T(8,128)S(1)} %reshape.216, s32[]{:T(128)S(6)} %select_n.11), kind=kOutput, calls=%fused_computation.26 | convolution fusion | flops 805306368 | bytes 4849668 | tf_op jit(solution)/shard_map/dot_general | solution.py:61
  16.8 0.0 all-reduce.2.cloned.1.call-update
  16.8 0.6 fusion.28
  17.4 0.1 copy.38
  17.5 5.8 %cholesky.16 = f32[64,64]{1,0:T(8,128)S(1)} custom-call(f32[64,64]{1,0:T(8,128)S(1)} %fusion.23), custom_call_target="Cholesky" | custom-call | tf_op jit(solution)/shard_map/jit(cholesky)/cholesky | solution.py:68
  23.4 0.6 compare_reduce_fusion
  24.0 0.7 fusion.18
  24.7 0.1 dynamic-slice
  24.8 4.9 %custom-call.10 = f32[1,64,64]{1,2,0:T(8,128)S(1)} custom-call(f32[1,64,64]{2,1,0:T(8,128)S(1)} %fusion.18), custom_call_target="InvertDiagBlocksLowerTriangular" | custom-call | tf_op jit(solution)/shard_map/jit(_cho_solve)/triangular_solve | solution.py:70
  29.7 1.4 convolution_bitcast_fusion.2
  31.1 21.8 %all-reduce.2.cloned.1.call-done = f32[64,2048]{1,0:T(8,128)} async-done(((f32[64,2048]{1,0:T(8,128)}), f32[64,2048]{1,0:T(8,128)}) %all-reduce.2.cloned.1.call-update) | async-done | bytes 524304 | tf_op jit(solution)/shard_map/psum | solution.py:69
  52.9 1.7 fusion.21
  54.6 0.6 fusion.19
  55.1 0.0 copy-start
  55.1 0.6 fusion.30
  55.7 6.6 %convolution_subtract_fusion = f32[2048,512]{1,0:T(8,128)} fusion(f32[2048,512]{1,0:T(8,128)} %param.4, f32[64,2048]{1,0:T(8,128)S(1)} %fusion.19, f32[64,2048]{1,0:T(8,128)S(1)} %reshape.216, s32[]{:T(128)S(6)} %select_n.11), kind=kOutput, calls=%fused_computation.1 | convolution fusion | flops 806354944 | bytes 9043972 | tf_op jit(solution)/shard_map/dot_general | solution.py:71
  62.3 0.0 copy-start.3
  62.4 0.0 copy-start.2
  62.4 1.1 reshape.219
  63.4 72.8 %psum.23 = f32[32,32,2,2]{3,1,2,0:T(8,128)S(1)} all-reduce(f32[32,32,2,2]{3,1,2,0:T(8,128)S(1)} %bitcast.63), channel_id=1, replica_groups=mesh['space'=8,'tm'=4] {'space'}, use_global_device_ids=true, to_apply=%region_4.5 | all-reduce | flops 4096 | bytes 32768 | tf_op jit(solution)/shard_map/psum | solution.py:90
  136.3 0.5 copy.42
  136.8 0.0 copy-done.3
  136.8 0.9 convolution_bitcast_fusion
  137.7 0.0 copy-done.2
  137.7 0.5 fusion.1
  138.1 0.5 copy.45
  138.6 1.3 reshape.221
  139.9 6.3 %fusion.10 = f32[2048,64]{0,1:T(8,128)S(1)} fusion(f32[2048,512]{1,0:T(8,128)} %convolution_subtract_fusion, f32[64,2048]{1,0:T(8,128)S(1)} %reshape.216, s32[]{:T(128)S(6)} %select_n.11, f32[512]{0:T(512)S(1)} %dynamic-slice), kind=kOutput, calls=%fused_computation.21 | convolution fusion | flops 805339136 | bytes 4851716 | tf_op jit(solution)/shard_map/dot_general | solution.py:79
  146.2 0.0 copy-done
  146.2 0.0 copy-start.1
  146.2 0.6 fusion.29
  146.8 1.1 reshape.217
  147.9 0.8 copy.39
  148.7 48.2 %psum.22 = f32[32,2,32,2]{3,1,2,0:T(2,128)S(1)} all-reduce(f32[32,2,32,2]{3,1,2,0:T(2,128)S(1)} %copy.39), channel_id=1, replica_groups=mesh['space'=8,'tm'=4] {'space','tm'}, use_global_device_ids=true, to_apply=%region_3.4 | all-reduce | flops 4096 | bytes 32768 | tf_op jit(solution)/shard_map/psum | solution.py:89
  197.0 0.7 gather_fusion
  197.6 0.0 copy-done.1
  197.6 0.1 fusion.2
  197.8 0.1 copy.41
  197.9 0.6 reshape.218
  (6 shorter events, 0.1 us)
Async XLA Ops:
  7.2 45.7 %all-reduce.2.cloned.1.call-start = ((), (), s32[]{:S(2)}) async-start(), calls=%async_computation | async-start | bytes 1048576 | tf_op jit(solution)/shard_map/psum | solution.py:69
  55.1 91.1 %copy-start = (f32[64,2048]{1,0:T(8,128)}, f32[64,2048]{1,0:T(8,128)S(1)}, u32[]{:S(2)}) copy-start(f32[64,2048]{1,0:T(8,128)S(1)} %fusion.19) | copy-start | bytes 1572868
  62.3 74.5 %copy-start.3 = (f32[2,2,2,1,1,1]{2,0,1,5,4,3:T(2,128)S(1)}, f32[2,2,2,1,1,1]{2,0,1,5,4,3:T(2,128)}, u32[]{:S(2)}) copy-start(f32[2,2,2,1,1,1]{2,0,1,5,4,3:T(2,128)} %constant.85) | copy-start | bytes 100
  62.4 75.3 %copy-start.2 = (f32[2,2,2,1,1]{2,0,1,4,3:T(2,128)S(1)}, f32[2,2,2,1,1]{2,0,1,4,3:T(2,128)}, u32[]{:S(2)}) copy-start(f32[2,2,2,1,1]{2,0,1,4,3:T(2,128)} %constant.86) | copy-start | bytes 100
  146.2 51.4 %copy-start.1 = (f32[2,2,2]{2,0,1:T(2,128)S(1)}, f32[2,2,2]{2,0,1:T(2,128)}, u32[]{:S(2)}) copy-start(f32[2,2,2]{2,0,1:T(2,128)} %constant.71.clone) | copy-start | bytes 100
Sparse Core Ops, SparseCore 0:
  17.0 35.8 all-reduce.1
where the time goes:
time: 206 us; the launch traced here: 205 us
  blocking collectives  121 us (59%)
  matrix products  26.8 us (13%)
  waiting for transfers between devices  21.8 us (11%)
  between operations  14.2 us (7%)
  other arithmetic  13.9 us (7%)
  local copies, waits for them, and re-layouts  7.49 us (4%)
    psum x1, blocking collectives, local(): mode_gram = lax.psum(outer_sum(spatial_modes, spatial_modes), 'space')  72.8 us
    psum x1, blocking collectives, local(): cross_term = lax.psum(cross_part, ('space', 'tm'))  48.2 us
    psum x1, waiting for transfers between devices, local(): projection = lax.psum(projection_part, 'tm')  21.8 us
    dot_general x1, matrix products, local(): lax.dot_general(epoch_vector_set, frame_slab, (((1,), (1,)), ((), ())), p...  7.05 us
    dot_general x1, matrix products, local(): lax.dot_general(spatial_modes, epoch_vector_set, (((0,), (0,)), ((), ()))...  6.63 us
    another operation x3, other arithmetic, local(): factor = jnp.linalg.cholesky(basis_gram)  6.52 us
    dot_general x1, matrix products, local(): lax.dot_general(misfit_matrix, jacobian_lines, (((1,), (1,)), ((), ())),...  6.35 us
    another operation x2, other arithmetic, local(): spatial_modes = jax.scipy.linalg.cho_solve((factor, True), projection)  5.55 us
  transfers between devices with their start and end apart: 1, of which 1 were waited for; matrix products, arithmetic and copies ran while one was open for 7% of the time, Pallas kernels for 0%

commit v1 on v0

v1 whole, which is shorter than its diff:
```python
import functools

import jax
import jax.numpy as jnp
from jax import lax
from jax.experimental import pallas as pl
from jax.experimental.pallas import tpu as pltpu
from jax.sharding import PartitionSpec as P

f32 = jnp.float32
bf16 = jnp.bfloat16
highest = lax.Precision.HIGHEST
NN = (((1,), (0,)), ((), ()))
NT = (((1,), (1,)), ((), ()))
TN = (((0,), (0,)), ((), ()))
MESH = pl.DeviceIdType.MESH
CHUNK = 256
HALF = CHUNK // 2
BLOCK = 128


def dot(a, b, dims, precision=None):
    return lax.dot_general(a, b, dims, precision=precision, preferred_element_type=f32)


def split(x):
    hi = x.astype(bf16)
    return hi, (x - hi.astype(f32)).astype(bf16)


def iota(shape, dim):
    return lax.broadcasted_iota(jnp.int32, shape, dim)


def kernel(
    n_space, n_tm, total_points,
    frame, rates, freqs,
    modes_out, misfit_out, grad_out, newton_out,
    slab, basis, slopes, part, modes, from_core, from_y, gram2, slope_gram, sums1, sums2,
    in_sem, out_sem, modes_sem, s1_send, s1_recv, y_send, y_recv, ag_send, ag_recv,
    p1_send, p1_recv, p2_send, p2_recv,
):
    points, epochs = slab.shape
    rows = 2 * rates.shape[1]
    chunks = points // CHUNK
    n_y = n_tm // 2
    total_epochs = epochs * n_tm
    share = rows // n_tm
    si, ti = lax.axis_index("space"), lax.axis_index("tm")
    yi, core = ti // 2, lax.rem(ti, 2)
    sibling = yi * 2 + (1 - core)

    def load(c):
        at = pl.ds(c * CHUNK, CHUNK)
        return pltpu.make_async_copy(frame.at[at], slab.at[at], in_sem.at[c])

    for c in range(chunks):
        load(c).start()

    space_peers = [lax.rem(si + d, n_space) for d in range(1, n_space)]
    tm_peers = [lax.rem(ti + d, n_tm) for d in range(1, n_tm)]
    barrier = pltpu.get_barrier_semaphore()
    for peer in space_peers:
        pl.semaphore_signal(barrier, inc=1, device_id={"space": peer}, device_id_type=MESH)
    for peer in tm_peers:
        pl.semaphore_signal(barrier, inc=1, device_id={"tm": peer}, device_id_type=MESH)

    pair_mask = iota((rows, rows // 2), 0) // 2 == iota((rows, rows // 2), 1)
    rate = jnp.sum(jnp.where(pair_mask, rates[...], 0.0), axis=1, keepdims=True)
    freq = jnp.sum(jnp.where(pair_mask, freqs[...], 0.0), axis=1, keepdims=True)
    lane = iota((rows, BLOCK), 1).astype(f32)
    even = lax.rem(iota((rows, BLOCK), 0), 2) == 0
    fine_t = lane / total_epochs
    coarse_t = lane * (BLOCK / total_epochs)
    fine_e = jnp.exp(rate * fine_t)
    fine_c = fine_e * jnp.cos(freq * fine_t)
    fine_s = fine_e * jnp.sin(freq * fine_t)
    coarse_e = jnp.exp(rate * jnp.minimum(coarse_t, 1.0))
    ca = coarse_e * jnp.cos(freq * coarse_t)
    sa = coarse_e * jnp.sin(freq * coarse_t)
    first = jnp.where(even, ca, sa)
    second = jnp.where(even, -sa, ca)
    for b in range(total_epochs // BLOCK):
        basis[:, b * BLOCK:(b + 1) * BLOCK] = (
            first[:, b:b + 1] * fine_c + second[:, b:b + 1] * fine_s
        )
    here = pl.ds(pl.multiple_of(ti * epochs, epochs), epochs)
    b_hi, b_lo = split(basis[:, here])
    b_two = jnp.concatenate([b_hi, b_lo], axis=0)
    pl.semaphore_wait(barrier, n_space + n_tm - 2)

    def half(c, who):
        return pl.ds(pl.multiple_of(c * CHUNK + who * HALF, HALF), HALF)

    def core_copy(c):
        return pltpu.make_async_remote_copy(
            part.at[:, half(c, 1 - core)], from_core.at[c], s1_send.at[c], s1_recv.at[c],
            device_id={"tm": sibling}, device_id_type=MESH)

    def y_copy(c, d, slot):
        peer = lax.rem(yi + d, n_y) * 2 + core
        return pltpu.make_async_remote_copy(
            from_y.at[c, slot], from_y.at[c, slot], y_send.at[c, d], y_recv.at[c, slot],
            device_id={"tm": peer}, device_id_type=MESH)

    def modes_copy(c, who):
        at = half(c, who)
        return pltpu.make_async_remote_copy(
            modes.at[:, at], modes.at[:, at], ag_send.at[c], ag_recv.at[c],
            device_id={"tm": sibling}, device_id_type=MESH)

    def pass_on(c):
        core_copy(c).wait_recv()
        from_y[c, yi] = part[:, half(c, core)] + from_core[c]
        for d in range(1, n_y):
            y_copy(c, d, yi).start()

    for c in range(chunks):
        load(c).wait()
        f_hi, f_lo = split(slab[c * CHUNK:(c + 1) * CHUNK, :])
        two = dot(b_two, f_hi, NT)
        part[:, c * CHUNK:(c + 1) * CHUNK] = (two[rows:] + dot(b_hi, f_lo, NT)) + two[:rows]
        core_copy(c).start()
        if c:
            pass_on(c - 1)
    pass_on(chunks - 1)

    gram = dot(basis[...], basis[...], NT, highest)
    eye = (iota((rows, rows), 0) == iota((rows, rows), 1)).astype(f32)
    aug = jnp.concatenate([gram, eye], axis=1)
    row_id = iota(aug.shape, 0)
    for k in range(rows):
        pivot = aug[k:k + 1, :] / aug[k:k + 1, k:k + 1]
        aug = jnp.where(row_id == k, pivot, aug - aug[:, k:k + 1] * pivot)
    inverse = aug[:, rows:]

    first2 = jnp.where(even, -sa, ca)
    second2 = jnp.where(even, -ca, -sa)
    for b in range(total_epochs // BLOCK):
        at = slice(b * BLOCK, (b + 1) * BLOCK)
        t = fine_t + b * (BLOCK / total_epochs)
        slopes[:rows, at] = basis[:, at] * t
        slopes[rows:, at] = (first2[:, b:b + 1] * fine_c + second2[:, b:b + 1] * fine_s) * t
    j_hi, j_lo = split(slopes[...])
    cross = dot(j_lo, j_hi, NT)
    slope_gram[...] = dot(j_hi, j_hi, NT) + (cross + cross.T)

    b_three = jnp.concatenate([b_hi, b_hi, b_lo], axis=0)
    moment = jnp.zeros((rows, epochs), f32)
    gram_two = jnp.zeros((2 * rows, rows), f32)

    def solve(c):
        for d in range(1, n_y):
            y_copy(c, d, lax.rem(yi + d, n_y)).wait_recv()
        total = from_y[c, 0]
        for y in range(1, n_y):
            total = total + from_y[c, y]
        modes[:, half(c, core)] = dot(inverse, total, NN, highest)
        modes_copy(c, core).start()

    def store(c):
        at = pl.ds(c * CHUNK, CHUNK)
        return (pltpu.make_async_copy(slab.at[at], misfit_out.at[at], out_sem.at[c]),
                pltpu.make_async_copy(modes.at[:, at], modes_out.at[:, at], modes_sem.at[c]))

    solve(0)
    for c in range(chunks):
        if c + 1 < chunks:
            solve(c + 1)
        modes_copy(c, 1 - core).wait_recv()
        at = slice(c * CHUNK, (c + 1) * CHUNK)
        s_hi, s_lo = split(modes[:, at])
        fitted = dot(jnp.concatenate([s_hi, s_lo, s_hi], axis=0), b_three, TN)
        misfit = slab[at, :] - fitted
        slab[at, :] = misfit
        for copy in store(c):
            copy.start()
        m_hi, m_lo = split(misfit)
        s_two = jnp.concatenate([s_hi, s_lo], axis=0)
        two = dot(s_two, m_hi, NN)
        moment = moment + ((two[rows:] + dot(s_hi, m_lo, NN)) + two[:rows])
        gram_two = gram_two + dot(s_two, s_hi, NT)

    low = gram_two[rows:]
    mode_gram = gram_two[:rows] + (low + low.T)
    gram2[...] = jnp.concatenate([mode_gram, mode_gram], axis=1)
    decay = jnp.sum(moment * slopes[:rows, here], axis=1, keepdims=True)
    turn = jnp.sum(moment * slopes[rows:, here], axis=1, keepdims=True)
    r64, c64 = iota((rows, rows), 0), iota((rows, rows), 1)
    picked = jnp.where(lax.rem(c64, 2) == 0, decay, turn)
    grad = jnp.sum(jnp.where(r64 // 2 == c64 // 2, picked, 0.0), axis=0, keepdims=True)
    zeros = jnp.zeros((7, 2 * rows), f32)
    wide = jnp.concatenate([grad, jnp.zeros_like(grad)], axis=1)
    mine = pl.ds(pl.multiple_of(ti * share, share), share)
    sums1[si, :share, :] = gram2[mine, :]
    sums1[si, share:, :] = jnp.concatenate([wide, zeros], axis=0)

    def copy1(d, slot):
        return pltpu.make_async_remote_copy(
            sums1.at[slot], sums1.at[slot], p1_send.at[d], p1_recv.at[slot],
            device_id={"space": lax.rem(si + d, n_space)}, device_id_type=MESH)

    def copy2(d, slot):
        return pltpu.make_async_remote_copy(
            sums2.at[slot], sums2.at[slot], p2_send.at[d], p2_recv.at[slot],
            device_id={"tm": lax.rem(ti + d, n_tm)}, device_id_type=MESH)

    for d in range(1, n_space):
        copy1(d, si).start()
    for d in range(1, n_space):
        copy1(d, lax.rem(si + d, n_space)).wait_recv()
    total = sums1[0]
    for s in range(1, n_space):
        total = total + sums1[s]
    scale = 1.0 / (total_points * total_epochs)
    below = pl.ds(pl.multiple_of(ti * share + rows, share), share)
    m2 = total[:share]
    both = jnp.concatenate([m2 * slope_gram[mine, :], m2 * slope_gram[below, :]], axis=0)
    u, v = iota((2 * rows, rows), 0), iota((2 * rows, rows), 1)
    take_cols = jnp.where((lax.rem(u, rows) // 2 == v // 2) & (u // rows == lax.rem(v, 2)), 1.0, 0.0)
    u, v = iota((share, 2 * share), 0), iota((share, 2 * share), 1)
    take_rows = jnp.where((lax.rem(v, share) // 2 == u // 2) & (v // share == lax.rem(u, 2)), 1.0, 0.0)
    newton = scale * dot(take_rows, dot(both, take_cols, NN, highest), NN, highest)
    sums2[ti, :share, :] = jnp.concatenate([newton, jnp.zeros_like(newton)], axis=1)
    sums2[ti, share:, :] = total[share:] * -scale
    for d in range(1, n_tm):
        copy2(d, ti).start()
    for d in range(1, n_tm):
        copy2(d, lax.rem(ti + d, n_tm)).wait_recv()
    gradient = sums2[0, share:share + 1, :rows]
    for j in range(n_tm):
        newton_out[j * share:(j + 1) * share, :] = sums2[j, :share, :rows]
        if j:
            gradient = gradient + sums2[j, share:share + 1, :rows]
    grad_out[...] = gradient

    for c in range(chunks):
        core_copy(c).wait_send()
        for d in range(1, n_y):
            y_copy(c, d, yi).wait_send()
        modes_copy(c, core).wait_send()
        for copy in store(c):
            copy.wait()
    for d in range(1, n_space):
        copy1(d, si).wait_send()
    for d in range(1, n_tm):
        copy2(d, ti).wait_send()


def local(n_space, n_tm, frame_slab, pair_decay_rates, pair_angular_frequencies):
    points, epochs = frame_slab.shape
    pairs = pair_decay_rates.shape[0]
    rows = 2 * pairs
    chunks = points // CHUNK
    n_y = n_tm // 2
    share = rows // n_tm
    any_space = pl.BlockSpec(memory_space=pl.ANY)
    vmem = pl.BlockSpec(memory_space=pltpu.VMEM)
    dma = pltpu.SemaphoreType.DMA
    modes, misfit, grad, newton = pl.pallas_call(
        functools.partial(kernel, n_space, n_tm, points * n_space),
        out_shape=(
            jax.ShapeDtypeStruct((rows, points), f32),
            jax.ShapeDtypeStruct((points, epochs), f32),
            jax.ShapeDtypeStruct((1, rows), f32),
            jax.ShapeDtypeStruct((rows, rows), f32),
        ),
        in_specs=[any_space, vmem, vmem],
        out_specs=(any_space, any_space, vmem, vmem),
        scratch_shapes=[
            pltpu.VMEM((points, epochs), f32),
            pltpu.VMEM((rows, epochs * n_tm), f32),
            pltpu.VMEM((2 * rows, epochs * n_tm), f32),
            pltpu.VMEM((rows, points), f32),
            pltpu.VMEM((rows, points), f32),
            pltpu.VMEM((chunks, rows, HALF), f32),
            pltpu.VMEM((chunks, n_y, rows, HALF), f32),
            pltpu.VMEM((rows, 2 * rows), f32),
            pltpu.VMEM((2 * rows, 2 * rows), f32),
            pltpu.VMEM((n_space, share + 8, 2 * rows), f32),
            pltpu.VMEM((n_tm, share + 8, 2 * rows), f32),
            dma((chunks,)), dma((chunks,)), dma((chunks,)),
            dma((chunks,)), dma((chunks,)),
            dma((chunks, n_y)), dma((chunks, n_y)),
            dma((chunks,)), dma((chunks,)),
            dma((n_space,)), dma((n_space,)),
            dma((n_tm,)), dma((n_tm,)),
        ],
        compiler_params=pltpu.CompilerParams(
            collective_id=0, has_side_effects=True, vmem_limit_bytes=48 * 2**20
        ),
    )(frame_slab, pair_decay_rates[None, :], pair_angular_frequencies[None, :])
    return modes, misfit, grad.reshape(rows), newton


def solution(mesh):
    return jax.shard_map(
        functools.partial(local, mesh.shape["space"], mesh.shape["tm"]),
        mesh=mesh,
        in_specs=(P("space", "tm"), P(), P()),
        out_specs=(P(None, "space"), P("space", "tm"), P(), P()),
        check_vma=False,
    )
```

time: 206 us -> 39.4 us (0.19)
  blocking collectives: 121 us -> 0 us
  Pallas kernels: 0 us -> 33.4 us
  matrix products: 26.8 us -> 0 us
  waiting for transfers between devices: 21.8 us -> 0 us
  other arithmetic: 13.9 us -> 0 us
  between operations: 14.2 us -> 0.65 us
  local copies, waits for them, and re-layouts: 7.49 us -> 5.24 us
    psum x2 -> x0, blocking collectives: 121 us -> none  [the longest x1 72.8 us: local(): mode_gram = lax.psum(outer_sum(spatial_modes, spatial_modes), 'space')]
    pallas_call x0 -> x1, Pallas kernels: none -> 33.4 us  [local(): pl.pallas_call(functools.partial(kernel, n_space, n_tm, points * n_space)...]
    dot_general x10 -> x0, matrix products: 24.6 us -> none  [the longest x1 7.05 us: local(): lax.dot_general(epoch_vector_set, frame_slab, (((1,), (1,)), ((), ())), p...]
    psum x1 -> x0, waiting for transfers between devices: 21.8 us -> none  [local(): projection = lax.psum(projection_part, 'tm')]
    another operation x6 -> x0, other arithmetic: 12.1 us -> none  [the longest x3 6.52 us: local(): factor = jnp.linalg.cholesky(basis_gram)]
    reshape x6 -> x0, local copies, waits for them, and re-layouts: 5.23 us -> none  [the longest x2 1.91 us: newton_terms(): cross_blocks = cross_term.reshape(pairs, 2, pairs, 2)]
    unnamed x8, local copies, waits for them, and re-layouts: 0.02 us -> 5.24 us
    another operation x2 -> x0, matrix products: 2.23 us -> none  [local(): spatial_modes = jax.scipy.linalg.cho_solve((factor, True), projection)]
  transfers between devices with their start and end apart: 1 -> 0, of which waited for: 1 -> 0; matrix products, arithmetic and copies ran while one was open for 7% -> 0% of each run, Pallas kernels for 0% -> 0%
where the time goes in v1:
time: 39.4 us; the launch traced here: 39.3 us
  Pallas kernels  33.4 us (85%)
  local copies, waits for them, and re-layouts  5.24 us (13%)
  between operations  0.65 us (2%)
    pallas_call x1, Pallas kernels, local(): pl.pallas_call(functools.partial(kernel, n_space, n_tm, points * n_space)...  33.4 us
    unnamed x8, local copies, waits for them, and re-layouts  5.24 us

profile of v1, /device:TPU:0, one launch (start us, length us, event | category | flops | bytes accessed | tf_op | source)
XLA Modules:
  0.0 39.3 jit_solution(3530598580664960331)
XLA Ops:
  0.6 0.0 copy-start
  0.6 0.6 %copy-done = f32[32]{0:T(128)S(1)} copy-done((f32[32]{0:T(128)S(1)}, f32[32]{0:T(128)}, u32[]{:S(2)}) %copy-start) | copy-done | bytes 152
  1.3 0.0 copy-start.1
  1.3 0.7 %copy-done.1 = f32[32]{0:T(128)S(1)} copy-done((f32[32]{0:T(128)S(1)}, f32[32]{0:T(128)}, u32[]{:S(2)}) %copy-start.1) | copy-done | bytes 152
  1.9 33.4 %shard_map.66 = (f32[64,2048]{1,0:T(8,128)S(1)}, f32[2048,512]{1,0:T(8,128)S(1)}, f32[1,64]{1,0:T(1,128)S(1)}, f32[64,64]{1,0:T(8,128)S(1)}) custom-call(f32[2048,512]{1,0:T(8,128)} %frame.1, f32[1,32]{1,0:T(1,128)S(1)} %bitcast.3, f32[1,32]{1,0:T(1,128)S(1)} %bitcast.4), custom_call_target="tpu_custom_call" | custom-call | tf_op jit(solution)/shard_map/pallas_call | solution.py:260
  35.3 0.8 %copy.11 = f32[64,2048]{1,0:T(8,128)} copy(f32[64,2048]{1,0:T(8,128)S(1)} %get-tuple-element.16) | data formatting | bytes 1048576
  36.1 2.0 %copy.12 = f32[2048,512]{1,0:T(8,128)} copy(f32[2048,512]{1,0:T(8,128)S(1)} %get-tuple-element.17) | data formatting | bytes 8388608
  38.1 0.5 %copy.13 = f32[64]{0:T(128)} copy(f32[64]{0:T(128)S(1)} %bitcast.5) | data formatting | bytes 512
  38.6 0.6 %copy.14 = f32[64,64]{1,0:T(8,128)} copy(f32[64,64]{1,0:T(8,128)S(1)} %get-tuple-element.19) | data formatting | bytes 32768
Async XLA Ops:
  0.6 0.7 %copy-start = (f32[32]{0:T(128)S(1)}, f32[32]{0:T(128)}, u32[]{:S(2)}) copy-start(f32[32]{0:T(128)} %param.4) | copy-start | bytes 388
  1.3 0.7 %copy-start.1 = (f32[32]{0:T(128)S(1)}, f32[32]{0:T(128)}, u32[]{:S(2)}) copy-start(f32[32]{0:T(128)} %param.5) | copy-start | bytes 388

commit v2 on v1

--- a/solution.py
+++ b/solution.py
@@ -16,6 +16,7 @@
 MESH = pl.DeviceIdType.MESH
 CHUNK = 256
 HALF = CHUNK // 2
+AHEAD = 2
 BLOCK = 128
 
 
@@ -34,10 +35,10 @@
 
 def kernel(
     n_space, n_tm, total_points,
-    frame, rates, freqs,
-    modes_out, misfit_out, grad_out, newton_out,
-    slab, basis, slopes, part, modes, from_core, from_y, gram2, slope_gram, sums1, sums2,
-    in_sem, out_sem, modes_sem, s1_send, s1_recv, y_send, y_recv, ag_send, ag_recv,
+    frame, rates_in, freqs_in,
+    modes, slab, grad_out, newton_out,
+    rates, freqs, basis, slopes, part, from_core, from_y, gram2, slope_gram, sums1, sums2,
+    in_sem, par_sem, s1_send, s1_recv, y_send, y_recv, ag_send, ag_recv,
     p1_send, p1_recv, p2_send, p2_recv,
 ):
     points, epochs = slab.shape
@@ -54,6 +55,10 @@
         at = pl.ds(c * CHUNK, CHUNK)
         return pltpu.make_async_copy(frame.at[at], slab.at[at], in_sem.at[c])
 
+    parameters = [pltpu.make_async_copy(rates_in, rates, par_sem.at[0]),
+                  pltpu.make_async_copy(freqs_in, freqs, par_sem.at[1])]
+    for copy in parameters:
+        copy.start()
     for c in range(chunks):
         load(c).start()
 
@@ -65,6 +70,8 @@
     for peer in tm_peers:
         pl.semaphore_signal(barrier, inc=1, device_id={"tm": peer}, device_id_type=MESH)
 
+    for copy in parameters:
+        copy.wait()
     pair_mask = iota((rows, rows // 2), 0) // 2 == iota((rows, rows // 2), 1)
     rate = jnp.sum(jnp.where(pair_mask, rates[...], 0.0), axis=1, keepdims=True)
     freq = jnp.sum(jnp.where(pair_mask, freqs[...], 0.0), axis=1, keepdims=True)
@@ -87,6 +94,26 @@
     here = pl.ds(pl.multiple_of(ti * epochs, epochs), epochs)
     b_hi, b_lo = split(basis[:, here])
     b_two = jnp.concatenate([b_hi, b_lo], axis=0)
+
+    gram = dot(basis[...], basis[...], NT, highest)
+    eye = (iota((rows, rows), 0) == iota((rows, rows), 1)).astype(f32)
+    augmented = jnp.concatenate([gram, eye], axis=1)
+    tiles = [augmented[i:i + 8] for i in range(0, rows, 8)]
+    row_id = iota((8, 2 * rows), 0)
+
+    def eliminate(k):
+        own, o = k // 8, k % 8
+        r0, r1 = tiles[own][o:o + 1], tiles[own][o + 1:o + 2]
+        a, b = r0[:, k:k + 1], r0[:, k + 1:k + 2]
+        c, d = r1[:, k:k + 1], r1[:, k + 1:k + 2]
+        scale = 1.0 / (a * d - b * c)
+        p0 = (d * r0 - b * r1) * scale
+        p1 = (a * r1 - c * r0) * scale
+        for i in range(len(tiles)):
+            t = tiles[i]
+            tiles[i] = t - t[:, k:k + 1] * p0 - t[:, k + 1:k + 2] * p1
+        tiles[own] = jnp.where(row_id == o, p0, jnp.where(row_id == o + 1, p1, tiles[own]))
+
     pl.semaphore_wait(barrier, n_space + n_tm - 2)
 
     def half(c, who):
@@ -120,19 +147,14 @@
         f_hi, f_lo = split(slab[c * CHUNK:(c + 1) * CHUNK, :])
         two = dot(b_two, f_hi, NT)
         part[:, c * CHUNK:(c + 1) * CHUNK] = (two[rows:] + dot(b_hi, f_lo, NT)) + two[:rows]
+        for k in range(rows * c // chunks, rows * (c + 1) // chunks, 2):
+            eliminate(k)
         core_copy(c).start()
         if c:
             pass_on(c - 1)
     pass_on(chunks - 1)
 
-    gram = dot(basis[...], basis[...], NT, highest)
-    eye = (iota((rows, rows), 0) == iota((rows, rows), 1)).astype(f32)
-    aug = jnp.concatenate([gram, eye], axis=1)
-    row_id = iota(aug.shape, 0)
-    for k in range(rows):
-        pivot = aug[k:k + 1, :] / aug[k:k + 1, k:k + 1]
-        aug = jnp.where(row_id == k, pivot, aug - aug[:, k:k + 1] * pivot)
-    inverse = aug[:, rows:]
+    inverse = jnp.concatenate(tiles, axis=0)[:, rows:]
 
     first2 = jnp.where(even, -sa, ca)
     second2 = jnp.where(even, -ca, -sa)
@@ -158,23 +180,17 @@
         modes[:, half(c, core)] = dot(inverse, total, NN, highest)
         modes_copy(c, core).start()
 
-    def store(c):
-        at = pl.ds(c * CHUNK, CHUNK)
-        return (pltpu.make_async_copy(slab.at[at], misfit_out.at[at], out_sem.at[c]),
-                pltpu.make_async_copy(modes.at[:, at], modes_out.at[:, at], modes_sem.at[c]))
-
-    solve(0)
+    for c in range(min(AHEAD, chunks)):
+        solve(c)
     for c in range(chunks):
-        if c + 1 < chunks:
-            solve(c + 1)
+        if c + AHEAD < chunks:
+            solve(c + AHEAD)
         modes_copy(c, 1 - core).wait_recv()
         at = slice(c * CHUNK, (c + 1) * CHUNK)
         s_hi, s_lo = split(modes[:, at])
         fitted = dot(jnp.concatenate([s_hi, s_lo, s_hi], axis=0), b_three, TN)
         misfit = slab[at, :] - fitted
         slab[at, :] = misfit
-        for copy in store(c):
-            copy.start()
         m_hi, m_lo = split(misfit)
         s_two = jnp.concatenate([s_hi, s_lo], axis=0)
         two = dot(s_two, m_hi, NN)
@@ -239,12 +255,22 @@
         for d in range(1, n_y):
             y_copy(c, d, yi).wait_send()
         modes_copy(c, core).wait_send()
-        for copy in store(c):
-            copy.wait()
     for d in range(1, n_space):
         copy1(d, si).wait_send()
     for d in range(1, n_tm):
         copy2(d, ti).wait_send()
+
+
+def write_out(modes, misfit, grad, newton, modes_out, misfit_out, grad_out, newton_out, sem):
+    points = misfit.shape[0]
+    pieces = [pl.ds(i * (points // 8), points // 8) for i in range(8)]
+    copies = [(misfit.at[p], misfit_out.at[p]) for p in pieces]
+    copies += [(modes, modes_out), (newton, newton_out), (grad, grad_out)]
+    copies = [pltpu.make_async_copy(a, b, sem.at[i]) for i, (a, b) in enumerate(copies)]
+    for copy in copies:
+        copy.start()
+    for copy in copies:
+        copy.wait()
 
 
 def local(n_space, n_tm, frame_slab, pair_decay_rates, pair_angular_frequencies):
@@ -254,24 +280,27 @@
     chunks = points // CHUNK
     n_y = n_tm // 2
     share = rows // n_tm
+    hbm = pl.BlockSpec(memory_space=pltpu.HBM)
     any_space = pl.BlockSpec(memory_space=pl.ANY)
     vmem = pl.BlockSpec(memory_space=pltpu.VMEM)
     dma = pltpu.SemaphoreType.DMA
-    modes, misfit, grad, newton = pl.pallas_call(
+    shapes = (
+        jax.ShapeDtypeStruct((rows, points), f32),
+        jax.ShapeDtypeStruct((points, epochs), f32),
+        jax.ShapeDtypeStruct((1, rows), f32),
+        jax.ShapeDtypeStruct((rows, rows), f32),
+    )
+    operands = (frame_slab, pair_decay_rates[None, :], pair_angular_frequencies[None, :])
+    results = pl.pallas_call(
         functools.partial(kernel, n_space, n_tm, points * n_space),
-        out_shape=(
-            jax.ShapeDtypeStruct((rows, points), f32),
-            jax.ShapeDtypeStruct((points, epochs), f32),
-            jax.ShapeDtypeStruct((1, rows), f32),
-            jax.ShapeDtypeStruct((rows, rows), f32),
-        ),
-        in_specs=[any_space, vmem, vmem],
-        out_specs=(any_space, any_space, vmem, vmem),
+        out_shape=shapes,
+        in_specs=[hbm] * 3,
+        out_specs=(vmem,) * 4,
         scratch_shapes=[
-            pltpu.VMEM((points, epochs), f32),
+            pltpu.VMEM((1, pairs), f32),
+            pltpu.VMEM((1, pairs), f32),
             pltpu.VMEM((rows, epochs * n_tm), f32),
             pltpu.VMEM((2 * rows, epochs * n_tm), f32),
-            pltpu.VMEM((rows, points), f32),
             pltpu.VMEM((rows, points), f32),
             pltpu.VMEM((chunks, rows, HALF), f32),
             pltpu.VMEM((chunks, n_y, rows, HALF), f32),
@@ -279,7 +308,7 @@
             pltpu.VMEM((2 * rows, 2 * rows), f32),
             pltpu.VMEM((n_space, share + 8, 2 * rows), f32),
             pltpu.VMEM((n_tm, share + 8, 2 * rows), f32),
-            dma((chunks,)), dma((chunks,)), dma((chunks,)),
+            dma((chunks,)), dma((2,)),
             dma((chunks,)), dma((chunks,)),
             dma((chunks, n_y)), dma((chunks, n_y)),
             dma((chunks,)), dma((chunks,)),
@@ -289,7 +318,14 @@
         compiler_params=pltpu.CompilerParams(
             collective_id=0, has_side_effects=True, vmem_limit_bytes=48 * 2**20
         ),
-    )(frame_slab, pair_decay_rates[None, :], pair_angular_frequencies[None, :])
+    )(*(pltpu.with_memory_space_constraint(x, pltpu.HBM) for x in operands))
+    modes, misfit, grad, newton = pl.pallas_call(
+        write_out,
+        out_shape=shapes,
+        in_specs=[any_space] * 4,
+        out_specs=(hbm,) * 4,
+        scratch_shapes=[dma((12,))],
+    )(*results)
     return modes, misfit, grad.reshape(rows), newton
 
 

time: 39.4 us -> 180 us (4.57)
  Pallas kernels: 33.4 us -> 175 us
    pallas_call x0 -> x1, Pallas kernels: none -> 145 us  [local(): pl.pallas_call(write_out, out_shape=shapes, in_specs=[any_space] * 4, out...]
    pallas_call x1, Pallas kernels: 33.4 us -> 29.6 us  [local(): pl.pallas_call(functools.partial(kernel, n_space, n_tm, points * n_space)...]
where the time goes in v2:
time: 180 us; the launch traced here: 179 us
  Pallas kernels  175 us (97%)
  local copies, waits for them, and re-layouts  3.92 us (2%)
    pallas_call x1, Pallas kernels, local(): pl.pallas_call(write_out, out_shape=shapes, in_specs=[any_space] * 4, out...  145 us
    pallas_call x1, Pallas kernels, local(): pl.pallas_call(functools.partial(kernel, n_space, n_tm, points * n_space)...  29.6 us
    unnamed x8, local copies, waits for them, and re-layouts  3.92 us

profile of v2, /device:TPU:0, one launch (start us, length us, event | category | flops | bytes accessed | tf_op | source)
XLA Modules:
  0.0 179.4 jit_solution(10383516499038254402)
XLA Ops:
  0.6 29.6 %shard_map.66 = (f32[64,2048]{1,0:T(8,128)S(1)}, f32[2048,512]{1,0:T(8,128)S(1)}, f32[1,64]{1,0:T(1,128)S(1)}, f32[64,64]{1,0:T(8,128)S(1)}) custom-call(f32[2048,512]{1,0:T(8,128)} %frame.1, f32[1,32]{1,0:T(1,128)} %bitcast.3, f32[1,32]{1,0:T(1,128)} %bitcast.4), custom_call_target="tpu_custom_call" | custom-call | tf_op jit(solution)/shard_map/pallas_call | solution.py:294
  30.3 0.0 copy-start
  30.3 1.9 %copy-done = f32[2048,512]{1,0:T(8,128)} copy-done((f32[2048,512]{1,0:T(8,128)}, f32[2048,512]{1,0:T(8,128)S(1)}, u32[]{:S(2)}) %copy-start) | copy-done | bytes 4194328
  32.2 0.0 copy-start.1
  32.2 0.8 copy-done.1
  33.0 0.0 copy-start.2
  33.0 0.6 copy-done.2
  33.6 0.0 copy-start.3
  33.6 0.6 copy-done.3
  34.2 145.2 %shard_map.67 = (f32[64,2048]{1,0:T(8,128)}, f32[2048,512]{1,0:T(8,128)}, f32[1,64]{1,0:T(1,128)}, f32[64,64]{1,0:T(8,128)}) custom-call(f32[64,2048]{1,0:T(8,128)} %copy-done.1, f32[2048,512]{1,0:T(8,128)} %copy-done, f32[1,64]{1,0:T(1,128)} %copy-done.3, f32[64,64]{1,0:T(8,128)} %copy-done.2), custom_call_target="tpu_custom_call" | custom-call | tf_op jit(solution)/shard_map/pallas_call | solution.py:322
Async XLA Ops:
  30.3 1.9 %copy-start = (f32[2048,512]{1,0:T(8,128)}, f32[2048,512]{1,0:T(8,128)S(1)}, u32[]{:S(2)}) copy-start(f32[2048,512]{1,0:T(8,128)S(1)} %get-tuple-element.13.misfit) | copy-start | bytes 12582916
  32.2 0.8 copy-start.1
  33.0 0.6 copy-start.2
  33.6 0.6 copy-start.3

commit v3 on v2

--- a/solution.py
+++ b/solution.py
@@ -16,7 +16,7 @@
 MESH = pl.DeviceIdType.MESH
 CHUNK = 256
 HALF = CHUNK // 2
-AHEAD = 2
+AHEAD = 6
 BLOCK = 128
 
 
@@ -31,15 +31,28 @@
 
 def iota(shape, dim):
     return lax.broadcasted_iota(jnp.int32, shape, dim)
+
+
+def cos_sin(x):
+    n = jnp.floor(x * 0.6366197723675814 + 0.5)
+    r = ((x - n * 1.5703125) - n * 0.0004837512969970703) - n * 7.549789948768648e-08
+    z = r * r
+    s = r + r * z * (-1.6666654611e-1 + z * (8.3321608736e-3 - z * 1.9515295891e-4))
+    c = 1.0 - 0.5 * z + z * z * (
+        4.166664568298827e-2 + z * (-1.388731625493765e-3 + z * 2.443315711809948e-5))
+    q = n.astype(jnp.int32) & 3
+    odd = (q & 1) == 1
+    cos, sin = jnp.where(odd, s, c), jnp.where(odd, c, s)
+    return (jnp.where((q == 1) | (q == 2), -cos, cos), jnp.where(q >= 2, -sin, sin))
 
 
 def kernel(
     n_space, n_tm, total_points,
     frame, rates_in, freqs_in,
     modes, slab, grad_out, newton_out,
-    rates, freqs, basis, slopes, part, from_core, from_y, gram2, slope_gram, sums1, sums2,
+    rates, freqs, basis, slopes, part, from_core, from_y, gram2, slope_gram, sums1, sums2, grads,
     in_sem, par_sem, s1_send, s1_recv, y_send, y_recv, ag_send, ag_recv,
-    p1_send, p1_recv, p2_send, p2_recv,
+    p1_send, p1_recv, p2_send, p2_recv, g_send, g_recv,
 ):
     points, epochs = slab.shape
     rows = 2 * rates.shape[1]
@@ -62,13 +75,20 @@
     for c in range(chunks):
         load(c).start()
 
-    space_peers = [lax.rem(si + d, n_space) for d in range(1, n_space)]
-    tm_peers = [lax.rem(ti + d, n_tm) for d in range(1, n_tm)]
+    devices = n_space * n_tm
+    me = si * n_tm + ti
+
+    def other(d):
+        peer = lax.rem(me + d, devices)
+        return (peer // n_tm, lax.rem(peer, n_tm))
+
     barrier = pltpu.get_barrier_semaphore()
-    for peer in space_peers:
-        pl.semaphore_signal(barrier, inc=1, device_id={"space": peer}, device_id_type=MESH)
-    for peer in tm_peers:
-        pl.semaphore_signal(barrier, inc=1, device_id={"tm": peer}, device_id_type=MESH)
+
+    def greet(d, carry):
+        pl.semaphore_signal(barrier, inc=1, device_id=other(d), device_id_type=MESH)
+        return carry
+
+    lax.fori_loop(1, devices, greet, 0)
 
     for copy in parameters:
         copy.wait()
@@ -80,11 +100,12 @@
     fine_t = lane / total_epochs
     coarse_t = lane * (BLOCK / total_epochs)
     fine_e = jnp.exp(rate * fine_t)
-    fine_c = fine_e * jnp.cos(freq * fine_t)
-    fine_s = fine_e * jnp.sin(freq * fine_t)
-    coarse_e = jnp.exp(rate * jnp.minimum(coarse_t, 1.0))
-    ca = coarse_e * jnp.cos(freq * coarse_t)
-    sa = coarse_e * jnp.sin(freq * coarse_t)
+    fine_c, fine_s = cos_sin(freq * fine_t)
+    fine_c, fine_s = fine_e * fine_c, fine_e * fine_s
+    coarse_t = jnp.minimum(coarse_t, 1.0)
+    coarse_e = jnp.exp(rate * coarse_t)
+    ca, sa = cos_sin(freq * coarse_t)
+    ca, sa = coarse_e * ca, coarse_e * sa
     first = jnp.where(even, ca, sa)
     second = jnp.where(even, -sa, ca)
     for b in range(total_epochs // BLOCK):
@@ -114,7 +135,7 @@
             tiles[i] = t - t[:, k:k + 1] * p0 - t[:, k + 1:k + 2] * p1
         tiles[own] = jnp.where(row_id == o, p0, jnp.where(row_id == o + 1, p1, tiles[own]))
 
-    pl.semaphore_wait(barrier, n_space + n_tm - 2)
+    pl.semaphore_wait(barrier, devices - 1)
 
     def half(c, who):
         return pl.ds(pl.multiple_of(c * CHUNK + who * HALF, HALF), HALF)
@@ -169,7 +190,6 @@
 
     b_three = jnp.concatenate([b_hi, b_hi, b_lo], axis=0)
     moment = jnp.zeros((rows, epochs), f32)
-    gram_two = jnp.zeros((2 * rows, rows), f32)
 
     def solve(c):
         for d in range(1, n_y):
@@ -180,75 +200,104 @@
         modes[:, half(c, core)] = dot(inverse, total, NN, highest)
         modes_copy(c, core).start()
 
-    for c in range(min(AHEAD, chunks)):
+    mine = pl.ds(pl.multiple_of(ti * share, share), share)
+    below = pl.ds(pl.multiple_of(ti * share + rows, share), share)
+    scale = 1.0 / (total_points * total_epochs)
+
+    def copy1(d, slot):
+        return pltpu.make_async_remote_copy(
+            sums1.at[slot], sums1.at[slot], p1_send.at[d], p1_recv.at[slot],
+            device_id={"space": lax.rem(si + d, n_space)}, device_id_type=MESH)
+
+    def copy2(d, slot):
+        return pltpu.make_async_remote_copy(
+            sums2.at[slot], sums2.at[slot], p2_send.at[d], p2_recv.at[slot],
+            device_id={"tm": lax.rem(ti + d, n_tm)}, device_id_type=MESH)
+
+    def copy3(d, slot):
+        return pltpu.make_async_remote_copy(
+            grads.at[slot], grads.at[slot], g_send.at[d], g_recv.at[slot],
+            device_id=other(d), device_id_type=MESH)
+
+    def send_mode_gram():
+        s_hi, s_lo = split(modes[...])
+        two = dot(jnp.concatenate([s_hi, s_lo], axis=0), s_hi, NT)
+        low = two[rows:]
+        mode_gram = two[:rows] + (low + low.T)
+        gram2[...] = jnp.concatenate([mode_gram, mode_gram], axis=1)
+        sums1[si] = gram2[mine, :]
+        for d in range(1, n_space):
+            copy1(d, si).start()
+
+    def send_newton():
+        for d in range(1, n_space):
+            copy1(d, lax.rem(si + d, n_space)).wait_recv()
+        m2 = sums1[0]
+        for s in range(1, n_space):
+            m2 = m2 + sums1[s]
+        both = jnp.concatenate([m2 * slope_gram[mine, :], m2 * slope_gram[below, :]], axis=0)
+        u, v = iota((2 * rows, rows), 0), iota((2 * rows, rows), 1)
+        take_cols = jnp.where(
+            (lax.rem(u, rows) // 2 == v // 2) & (u // rows == lax.rem(v, 2)), 1.0, 0.0)
+        u, v = iota((share, 2 * share), 0), iota((share, 2 * share), 1)
+        take_rows = jnp.where(
+            (lax.rem(v, share) // 2 == u // 2) & (v // share == lax.rem(u, 2)), 1.0, 0.0)
+        newton = scale * dot(take_rows, dot(both, take_cols, NN, highest), NN, highest)
+        sums2[ti] = jnp.concatenate([newton, jnp.zeros_like(newton)], axis=1)
+        for d in range(1, n_tm):
+            copy2(d, ti).start()
+
+    ahead = min(AHEAD, chunks)
+    gram_at = min(chunks - ahead + 1, chunks - 1)
+    newton_at = max(chunks - 2, gram_at)
+    waited = 0
+    for c in range(ahead):
         solve(c)
     for c in range(chunks):
-        if c + AHEAD < chunks:
-            solve(c + AHEAD)
-        modes_copy(c, 1 - core).wait_recv()
+        if c + ahead < chunks:
+            solve(c + ahead)
+        need = chunks if c >= gram_at else c + 1
+        while waited < need:
+            modes_copy(waited, 1 - core).wait_recv()
+            waited += 1
+        if c == gram_at:
+            send_mode_gram()
+        if c == newton_at:
+            send_newton()
         at = slice(c * CHUNK, (c + 1) * CHUNK)
         s_hi, s_lo = split(modes[:, at])
         fitted = dot(jnp.concatenate([s_hi, s_lo, s_hi], axis=0), b_three, TN)
         misfit = slab[at, :] - fitted
         slab[at, :] = misfit
         m_hi, m_lo = split(misfit)
-        s_two = jnp.concatenate([s_hi, s_lo], axis=0)
-        two = dot(s_two, m_hi, NN)
+        two = dot(jnp.concatenate([s_hi, s_lo], axis=0), m_hi, NN)
         moment = moment + ((two[rows:] + dot(s_hi, m_lo, NN)) + two[:rows])
-        gram_two = gram_two + dot(s_two, s_hi, NT)
-
-    low = gram_two[rows:]
-    mode_gram = gram_two[:rows] + (low + low.T)
-    gram2[...] = jnp.concatenate([mode_gram, mode_gram], axis=1)
+
     decay = jnp.sum(moment * slopes[:rows, here], axis=1, keepdims=True)
     turn = jnp.sum(moment * slopes[rows:, here], axis=1, keepdims=True)
-    r64, c64 = iota((rows, rows), 0), iota((rows, rows), 1)
-    picked = jnp.where(lax.rem(c64, 2) == 0, decay, turn)
-    grad = jnp.sum(jnp.where(r64 // 2 == c64 // 2, picked, 0.0), axis=0, keepdims=True)
-    zeros = jnp.zeros((7, 2 * rows), f32)
-    wide = jnp.concatenate([grad, jnp.zeros_like(grad)], axis=1)
-    mine = pl.ds(pl.multiple_of(ti * share, share), share)
-    sums1[si, :share, :] = gram2[mine, :]
-    sums1[si, share:, :] = jnp.concatenate([wide, zeros], axis=0)
-
-    def copy1(d, slot):
-        return pltpu.make_async_remote_copy(
-            sums1.at[slot], sums1.at[slot], p1_send.at[d], p1_recv.at[slot],
-            device_id={"space": lax.rem(si + d, n_space)}, device_id_type=MESH)
-
-    def copy2(d, slot):
-        return pltpu.make_async_remote_copy(
-            sums2.at[slot], sums2.at[slot], p2_send.at[d], p2_recv.at[slot],
-            device_id={"tm": lax.rem(ti + d, n_tm)}, device_id_type=MESH)
-
-    for d in range(1, n_space):
-        copy1(d, si).start()
-    for d in range(1, n_space):
-        copy1(d, lax.rem(si + d, n_space)).wait_recv()
-    total = sums1[0]
-    for s in range(1, n_space):
-        total = total + sums1[s]
-    scale = 1.0 / (total_points * total_epochs)
-    below = pl.ds(pl.multiple_of(ti * share + rows, share), share)
-    m2 = total[:share]
-    both = jnp.concatenate([m2 * slope_gram[mine, :], m2 * slope_gram[below, :]], axis=0)
-    u, v = iota((2 * rows, rows), 0), iota((2 * rows, rows), 1)
-    take_cols = jnp.where((lax.rem(u, rows) // 2 == v // 2) & (u // rows == lax.rem(v, 2)), 1.0, 0.0)
-    u, v = iota((share, 2 * share), 0), iota((share, 2 * share), 1)
-    take_rows = jnp.where((lax.rem(v, share) // 2 == u // 2) & (v // share == lax.rem(u, 2)), 1.0, 0.0)
-    newton = scale * dot(take_rows, dot(both, take_cols, NN, highest), NN, highest)
-    sums2[ti, :share, :] = jnp.concatenate([newton, jnp.zeros_like(newton)], axis=1)
-    sums2[ti, share:, :] = total[share:] * -scale
-    for d in range(1, n_tm):
-        copy2(d, ti).start()
+    u, v = iota((rows, 2 * rows), 0), iota((rows, 2 * rows), 1)
+    picked = jnp.where(lax.rem(v, 2) == 0, decay, turn)
+    grads[me] = jnp.sum(jnp.where(u // 2 == v // 2, picked, 0.0), axis=0, keepdims=True)
+
+    def send_grad(d, carry):
+        copy3(d, me).start()
+        return carry
+
+    def take_grad(d, carry):
+        copy3(d, lax.rem(me + d, devices)).wait_recv()
+        return carry
+
+    def sent_grad(d, carry):
+        copy3(d, me).wait_send()
+        return carry
+
+    lax.fori_loop(1, devices, send_grad, 0)
     for d in range(1, n_tm):
         copy2(d, lax.rem(ti + d, n_tm)).wait_recv()
-    gradient = sums2[0, share:share + 1, :rows]
     for j in range(n_tm):
-        newton_out[j * share:(j + 1) * share, :] = sums2[j, :share, :rows]
-        if j:
-            gradient = gradient + sums2[j, share:share + 1, :rows]
-    grad_out[...] = gradient
+        newton_out[j * share:(j + 1) * share, :] = sums2[j, :, :rows]
+    lax.fori_loop(1, devices, take_grad, 0)
+    grad_out[...] = jnp.sum(grads[...], axis=0)[:, :rows] * -scale
 
     for c in range(chunks):
         core_copy(c).wait_send()
@@ -259,6 +308,7 @@
         copy1(d, si).wait_send()
     for d in range(1, n_tm):
         copy2(d, ti).wait_send()
+    lax.fori_loop(1, devices, sent_grad, 0)
 
 
 def write_out(modes, misfit, grad, newton, modes_out, misfit_out, grad_out, newton_out, sem):
@@ -281,7 +331,6 @@
     n_y = n_tm // 2
     share = rows // n_tm
     hbm = pl.BlockSpec(memory_space=pltpu.HBM)
-    any_space = pl.BlockSpec(memory_space=pl.ANY)
     vmem = pl.BlockSpec(memory_space=pltpu.VMEM)
     dma = pltpu.SemaphoreType.DMA
     shapes = (
@@ -306,14 +355,16 @@
             pltpu.VMEM((chunks, n_y, rows, HALF), f32),
             pltpu.VMEM((rows, 2 * rows), f32),
             pltpu.VMEM((2 * rows, 2 * rows), f32),
-            pltpu.VMEM((n_space, share + 8, 2 * rows), f32),
-            pltpu.VMEM((n_tm, share + 8, 2 * rows), f32),
+            pltpu.VMEM((n_space, share, 2 * rows), f32),
+            pltpu.VMEM((n_tm, share, 2 * rows), f32),
+            pltpu.VMEM((n_space * n_tm, 1, 2 * rows), f32),
             dma((chunks,)), dma((2,)),
             dma((chunks,)), dma((chunks,)),
             dma((chunks, n_y)), dma((chunks, n_y)),
             dma((chunks,)), dma((chunks,)),
             dma((n_space,)), dma((n_space,)),
             dma((n_tm,)), dma((n_tm,)),
+            dma((n_space * n_tm,)), dma((n_space * n_tm,)),
         ],
         compiler_params=pltpu.CompilerParams(
             collective_id=0, has_side_effects=True, vmem_limit_bytes=48 * 2**20
@@ -322,7 +373,7 @@
     modes, misfit, grad, newton = pl.pallas_call(
         write_out,
         out_shape=shapes,
-        in_specs=[any_space] * 4,
+        in_specs=[vmem] * 4,
         out_specs=(hbm,) * 4,
         scratch_shapes=[dma((12,))],
     )(*results)

time: 180 us -> 40.8 us (0.23)
  Pallas kernels: 175 us -> 36.1 us
    pallas_call x1, Pallas kernels: 145 us -> 4.59 us  [local(): pl.pallas_call(write_out, out_shape=shapes, in_specs=[vmem] * 4, out_spec...]
    pallas_call x1, Pallas kernels: 29.6 us -> 31.5 us  [local(): pl.pallas_call(functools.partial(kernel, n_space, n_tm, points * n_space)...]
where the time goes in v3:
time: 40.8 us; the launch traced here: 40.6 us
  Pallas kernels  36.1 us (88%)
  local copies, waits for them, and re-layouts  3.92 us (10%)
  between operations  0.65 us (2%)
    pallas_call x1, Pallas kernels, local(): pl.pallas_call(functools.partial(kernel, n_space, n_tm, points * n_space)...  31.5 us
    pallas_call x1, Pallas kernels, local(): pl.pallas_call(write_out, out_shape=shapes, in_specs=[vmem] * 4, out_spec...  4.59 us
    unnamed x8, local copies, waits for them, and re-layouts  3.92 us

profile of v3, /device:TPU:0, one launch (start us, length us, event | category | flops | bytes accessed | tf_op | source)
XLA Modules:
  0.0 40.6 jit_solution(4116977790721095443)
XLA Ops:
  0.6 31.5 %shard_map.66 = (f32[64,2048]{1,0:T(8,128)S(1)}, f32[2048,512]{1,0:T(8,128)S(1)}, f32[1,64]{1,0:T(1,128)S(1)}, f32[64,64]{1,0:T(8,128)S(1)}) custom-call(f32[2048,512]{1,0:T(8,128)} %frame.1, f32[1,32]{1,0:T(1,128)} %bitcast.3, f32[1,32]{1,0:T(1,128)} %bitcast.4), custom_call_target="tpu_custom_call" | custom-call | tf_op jit(solution)/shard_map/pallas_call | solution.py:343
  32.1 0.0 copy-start
  32.1 1.9 %copy-done = f32[2048,512]{1,0:T(8,128)} copy-done((f32[2048,512]{1,0:T(8,128)}, f32[2048,512]{1,0:T(8,128)S(1)}, u32[]{:S(2)}) %copy-start) | copy-done | bytes 4194328
  34.1 0.0 copy-start.1
  34.1 0.8 %copy-done.1 = f32[64,2048]{1,0:T(8,128)} copy-done((f32[64,2048]{1,0:T(8,128)}, f32[64,2048]{1,0:T(8,128)S(1)}, u32[]{:S(2)}) %copy-start.1) | copy-done | bytes 524312
  34.9 0.0 copy-start.2
  34.9 0.6 %copy-done.2 = f32[64,64]{1,0:T(8,128)} copy-done((f32[64,64]{1,0:T(8,128)}, f32[64,64]{1,0:T(8,128)S(1)}, u32[]{:S(2)}) %copy-start.2) | copy-done | bytes 16408
  35.5 0.0 copy-start.3
  35.5 0.6 %copy-done.3 = f32[1,64]{1,0:T(1,128)} copy-done((f32[1,64]{1,0:T(1,128)}, f32[1,64]{1,0:T(1,128)S(1)}, u32[]{:S(2)}) %copy-start.3) | copy-done | bytes 280
  36.0 4.6 %shard_map.67 = (f32[64,2048]{1,0:T(8,128)}, f32[2048,512]{1,0:T(8,128)}, f32[1,64]{1,0:T(1,128)}, f32[64,64]{1,0:T(8,128)}) custom-call(f32[64,2048]{1,0:T(8,128)} %copy-done.1, f32[2048,512]{1,0:T(8,128)} %copy-done, f32[1,64]{1,0:T(1,128)} %copy-done.3, f32[64,64]{1,0:T(8,128)} %copy-done.2), custom_call_target="tpu_custom_call" | custom-call | tf_op jit(solution)/shard_map/pallas_call | solution.py:373
Async XLA Ops:
  32.1 1.9 %copy-start = (f32[2048,512]{1,0:T(8,128)}, f32[2048,512]{1,0:T(8,128)S(1)}, u32[]{:S(2)}) copy-start(f32[2048,512]{1,0:T(8,128)S(1)} %get-tuple-element.13.misfit) | copy-start | bytes 12582916
  34.1 0.8 %copy-start.1 = (f32[64,2048]{1,0:T(8,128)}, f32[64,2048]{1,0:T(8,128)S(1)}, u32[]{:S(2)}) copy-start(f32[64,2048]{1,0:T(8,128)S(1)} %get-tuple-element.12.modes) | copy-start | bytes 1572868
  34.9 0.6 %copy-start.2 = (f32[64,64]{1,0:T(8,128)}, f32[64,64]{1,0:T(8,128)S(1)}, u32[]{:S(2)}) copy-start(f32[64,64]{1,0:T(8,128)S(1)} %get-tuple-element.15.newton) | copy-start | bytes 49156
  35.5 0.6 %copy-start.3 = (f32[1,64]{1,0:T(1,128)}, f32[1,64]{1,0:T(1,128)S(1)}, u32[]{:S(2)}) copy-start(f32[1,64]{1,0:T(1,128)S(1)} %get-tuple-element.14.grad) | copy-start | bytes 772

commit v4 on v3

--- a/solution.py
+++ b/solution.py
@@ -16,7 +16,8 @@
 MESH = pl.DeviceIdType.MESH
 CHUNK = 256
 HALF = CHUNK // 2
-AHEAD = 6
+AHEAD = 4
+LAG = 2
 BLOCK = 128
 
 
@@ -50,9 +51,10 @@
     n_space, n_tm, total_points,
     frame, rates_in, freqs_in,
     modes, slab, grad_out, newton_out,
-    rates, freqs, basis, slopes, part, from_core, from_y, gram2, slope_gram, sums1, sums2, grads,
+    rates, freqs, basis, slopes, part, from_core, from_y, gram2, slope_gram, sums1, sums2, grads1, grads2,
     in_sem, par_sem, s1_send, s1_recv, y_send, y_recv, ag_send, ag_recv,
-    p1_send, p1_recv, p2_send, p2_recv, g_send, g_recv,
+    p1_send, p1_recv, p2_send, p2_recv,
+    g1_send, g1_recv, g2_send, g2_recv,
 ):
     points, epochs = slab.shape
     rows = 2 * rates.shape[1]
@@ -75,20 +77,13 @@
     for c in range(chunks):
         load(c).start()
 
-    devices = n_space * n_tm
-    me = si * n_tm + ti
-
-    def other(d):
-        peer = lax.rem(me + d, devices)
-        return (peer // n_tm, lax.rem(peer, n_tm))
-
     barrier = pltpu.get_barrier_semaphore()
-
-    def greet(d, carry):
-        pl.semaphore_signal(barrier, inc=1, device_id=other(d), device_id_type=MESH)
-        return carry
-
-    lax.fori_loop(1, devices, greet, 0)
+    for d in range(1, n_space):
+        pl.semaphore_signal(barrier, inc=1, device_id={"space": lax.rem(si + d, n_space)},
+                            device_id_type=MESH)
+    for d in range(1, n_tm):
+        pl.semaphore_signal(barrier, inc=1, device_id={"tm": lax.rem(ti + d, n_tm)},
+                            device_id_type=MESH)
 
     for copy in parameters:
         copy.wait()
@@ -135,7 +130,7 @@
             tiles[i] = t - t[:, k:k + 1] * p0 - t[:, k + 1:k + 2] * p1
         tiles[own] = jnp.where(row_id == o, p0, jnp.where(row_id == o + 1, p1, tiles[own]))
 
-    pl.semaphore_wait(barrier, devices - 1)
+    pl.semaphore_wait(barrier, n_space + n_tm - 2)
 
     def half(c, who):
         return pl.ds(pl.multiple_of(c * CHUNK + who * HALF, HALF), HALF)
@@ -163,30 +158,34 @@
         for d in range(1, n_y):
             y_copy(c, d, yi).start()
 
+    first2 = jnp.where(even, -sa, ca)
+    second2 = jnp.where(even, -ca, -sa)
+
+    def slope_block(b):
+        at = slice(b * BLOCK, (b + 1) * BLOCK)
+        t = fine_t + b * (BLOCK / total_epochs)
+        slopes[:rows, at] = basis[:, at] * t
+        slopes[rows:, at] = (first2[:, b:b + 1] * fine_c + second2[:, b:b + 1] * fine_s) * t
+
+    blocks = total_epochs // BLOCK
     for c in range(chunks):
         load(c).wait()
         f_hi, f_lo = split(slab[c * CHUNK:(c + 1) * CHUNK, :])
         two = dot(b_two, f_hi, NT)
         part[:, c * CHUNK:(c + 1) * CHUNK] = (two[rows:] + dot(b_hi, f_lo, NT)) + two[:rows]
+        core_copy(c).start()
         for k in range(rows * c // chunks, rows * (c + 1) // chunks, 2):
             eliminate(k)
-        core_copy(c).start()
-        if c:
-            pass_on(c - 1)
-    pass_on(chunks - 1)
-
-    inverse = jnp.concatenate(tiles, axis=0)[:, rows:]
-
-    first2 = jnp.where(even, -sa, ca)
-    second2 = jnp.where(even, -ca, -sa)
-    for b in range(total_epochs // BLOCK):
-        at = slice(b * BLOCK, (b + 1) * BLOCK)
-        t = fine_t + b * (BLOCK / total_epochs)
-        slopes[:rows, at] = basis[:, at] * t
-        slopes[rows:, at] = (first2[:, b:b + 1] * fine_c + second2[:, b:b + 1] * fine_s) * t
+        for b in range(blocks * c // chunks, blocks * (c + 1) // chunks):
+            slope_block(b)
+        if c >= LAG:
+            pass_on(c - LAG)
+    for c in range(max(chunks - LAG, 0), chunks):
+        pass_on(c)
     j_hi, j_lo = split(slopes[...])
     cross = dot(j_lo, j_hi, NT)
     slope_gram[...] = dot(j_hi, j_hi, NT) + (cross + cross.T)
+    inverse = jnp.concatenate(tiles, axis=0)[:, rows:]
 
     b_three = jnp.concatenate([b_hi, b_hi, b_lo], axis=0)
     moment = jnp.zeros((rows, epochs), f32)
@@ -216,8 +215,13 @@
 
     def copy3(d, slot):
         return pltpu.make_async_remote_copy(
-            grads.at[slot], grads.at[slot], g_send.at[d], g_recv.at[slot],
-            device_id=other(d), device_id_type=MESH)
+            grads1.at[slot], grads1.at[slot], g1_send.at[d], g1_recv.at[slot],
+            device_id={"space": lax.rem(si + d, n_space)}, device_id_type=MESH)
+
+    def copy4(d, slot):
+        return pltpu.make_async_remote_copy(
+            grads2.at[slot], grads2.at[slot], g2_send.at[d], g2_recv.at[slot],
+            device_id={"tm": lax.rem(ti + d, n_tm)}, device_id_type=MESH)
 
     def send_mode_gram():
         s_hi, s_lo = split(modes[...])
@@ -249,7 +253,6 @@
 
     ahead = min(AHEAD, chunks)
     gram_at = min(chunks - ahead + 1, chunks - 1)
-    newton_at = max(chunks - 2, gram_at)
     waited = 0
     for c in range(ahead):
         solve(c)
@@ -262,8 +265,6 @@
             waited += 1
         if c == gram_at:
             send_mode_gram()
-        if c == newton_at:
-            send_newton()
         at = slice(c * CHUNK, (c + 1) * CHUNK)
         s_hi, s_lo = split(modes[:, at])
         fitted = dot(jnp.concatenate([s_hi, s_lo, s_hi], axis=0), b_three, TN)
@@ -277,27 +278,22 @@
     turn = jnp.sum(moment * slopes[rows:, here], axis=1, keepdims=True)
     u, v = iota((rows, 2 * rows), 0), iota((rows, 2 * rows), 1)
     picked = jnp.where(lax.rem(v, 2) == 0, decay, turn)
-    grads[me] = jnp.sum(jnp.where(u // 2 == v // 2, picked, 0.0), axis=0, keepdims=True)
-
-    def send_grad(d, carry):
-        copy3(d, me).start()
-        return carry
-
-    def take_grad(d, carry):
-        copy3(d, lax.rem(me + d, devices)).wait_recv()
-        return carry
-
-    def sent_grad(d, carry):
-        copy3(d, me).wait_send()
-        return carry
-
-    lax.fori_loop(1, devices, send_grad, 0)
+    grads1[si] = jnp.sum(jnp.where(u // 2 == v // 2, picked, 0.0), axis=0, keepdims=True)
+    for d in range(1, n_space):
+        copy3(d, si).start()
+    send_newton()
+    for d in range(1, n_space):
+        copy3(d, lax.rem(si + d, n_space)).wait_recv()
+    grads2[ti] = jnp.sum(grads1[...], axis=0)
+    for d in range(1, n_tm):
+        copy4(d, ti).start()
     for d in range(1, n_tm):
         copy2(d, lax.rem(ti + d, n_tm)).wait_recv()
     for j in range(n_tm):
         newton_out[j * share:(j + 1) * share, :] = sums2[j, :, :rows]
-    lax.fori_loop(1, devices, take_grad, 0)
-    grad_out[...] = jnp.sum(grads[...], axis=0)[:, :rows] * -scale
+    for d in range(1, n_tm):
+        copy4(d, lax.rem(ti + d, n_tm)).wait_recv()
+    grad_out[...] = jnp.sum(grads2[...], axis=0)[:, :rows] * -scale
 
     for c in range(chunks):
         core_copy(c).wait_send()
@@ -306,21 +302,10 @@
         modes_copy(c, core).wait_send()
     for d in range(1, n_space):
         copy1(d, si).wait_send()
+        copy3(d, si).wait_send()
     for d in range(1, n_tm):
         copy2(d, ti).wait_send()
-    lax.fori_loop(1, devices, sent_grad, 0)
-
-
-def write_out(modes, misfit, grad, newton, modes_out, misfit_out, grad_out, newton_out, sem):
-    points = misfit.shape[0]
-    pieces = [pl.ds(i * (points // 8), points // 8) for i in range(8)]
-    copies = [(misfit.at[p], misfit_out.at[p]) for p in pieces]
-    copies += [(modes, modes_out), (newton, newton_out), (grad, grad_out)]
-    copies = [pltpu.make_async_copy(a, b, sem.at[i]) for i, (a, b) in enumerate(copies)]
-    for copy in copies:
-        copy.start()
-    for copy in copies:
-        copy.wait()
+        copy4(d, ti).wait_send()
 
 
 def local(n_space, n_tm, frame_slab, pair_decay_rates, pair_angular_frequencies):
@@ -340,7 +325,7 @@
         jax.ShapeDtypeStruct((rows, rows), f32),
     )
     operands = (frame_slab, pair_decay_rates[None, :], pair_angular_frequencies[None, :])
-    results = pl.pallas_call(
+    modes, misfit, grad, newton = pl.pallas_call(
         functools.partial(kernel, n_space, n_tm, points * n_space),
         out_shape=shapes,
         in_specs=[hbm] * 3,
@@ -357,26 +342,21 @@
             pltpu.VMEM((2 * rows, 2 * rows), f32),
             pltpu.VMEM((n_space, share, 2 * rows), f32),
             pltpu.VMEM((n_tm, share, 2 * rows), f32),
-            pltpu.VMEM((n_space * n_tm, 1, 2 * rows), f32),
+            pltpu.VMEM((n_space, 1, 2 * rows), f32),
+            pltpu.VMEM((n_tm, 1, 2 * rows), f32),
             dma((chunks,)), dma((2,)),
             dma((chunks,)), dma((chunks,)),
             dma((chunks, n_y)), dma((chunks, n_y)),
             dma((chunks,)), dma((chunks,)),
             dma((n_space,)), dma((n_space,)),
             dma((n_tm,)), dma((n_tm,)),
-            dma((n_space * n_tm,)), dma((n_space * n_tm,)),
+            dma((n_space,)), dma((n_space,)),
+            dma((n_tm,)), dma((n_tm,)),
         ],
         compiler_params=pltpu.CompilerParams(
             collective_id=0, has_side_effects=True, vmem_limit_bytes=48 * 2**20
         ),
     )(*(pltpu.with_memory_space_constraint(x, pltpu.HBM) for x in operands))
-    modes, misfit, grad, newton = pl.pallas_call(
-        write_out,
-        out_shape=shapes,
-        in_specs=[vmem] * 4,
-        out_specs=(hbm,) * 4,
-        scratch_shapes=[dma((12,))],
-    )(*results)
     return modes, misfit, grad.reshape(rows), newton
 
 

time: 40.8 us -> 33.4 us (0.82)
  Pallas kernels: 36.1 us -> 28.6 us
    pallas_call x1 -> x0, Pallas kernels: 4.59 us -> none  [local(): pl.pallas_call(write_out, out_shape=shapes, in_specs=[vmem] * 4, out_spec...]
    pallas_call x1, Pallas kernels: 31.5 us -> 28.6 us  [local(): pl.pallas_call(functools.partial(kernel, n_space, n_tm, points * n_space)...]
    unnamed x8 -> x4, local copies, waits for them, and re-layouts: 3.92 us -> 3.93 us
where the time goes in v4:
time: 33.4 us; the launch traced here: 33.2 us
  Pallas kernels  28.6 us (86%)
  local copies, waits for them, and re-layouts  3.93 us (12%)
  between operations  0.64 us (2%)
    pallas_call x1, Pallas kernels, local(): pl.pallas_call(functools.partial(kernel, n_space, n_tm, points * n_space)...  28.6 us
    unnamed x4, local copies, waits for them, and re-layouts  3.93 us

profile of v4, /device:TPU:0, one launch (start us, length us, event | category | flops | bytes accessed | tf_op | source)
XLA Modules:
  0.0 33.2 jit_solution(11103677168726164886)
XLA Ops:
  0.6 28.6 %shard_map.66 = (f32[64,2048]{1,0:T(8,128)S(1)}, f32[2048,512]{1,0:T(8,128)S(1)}, f32[1,64]{1,0:T(1,128)S(1)}, f32[64,64]{1,0:T(8,128)S(1)}) custom-call(f32[2048,512]{1,0:T(8,128)} %frame.1, f32[1,32]{1,0:T(1,128)} %bitcast.4, f32[1,32]{1,0:T(1,128)} %bitcast.5), custom_call_target="tpu_custom_call" | custom-call | tf_op jit(solution)/shard_map/pallas_call | solution.py:328
  29.3 0.8 %copy.11 = f32[64,2048]{1,0:T(8,128)} copy(f32[64,2048]{1,0:T(8,128)S(1)} %get-tuple-element.16) | data formatting | bytes 1048576
  30.1 2.0 %copy.12 = f32[2048,512]{1,0:T(8,128)} copy(f32[2048,512]{1,0:T(8,128)S(1)} %get-tuple-element.17) | data formatting | bytes 8388608
  32.1 0.5 %copy.13 = f32[64]{0:T(128)} copy(f32[64]{0:T(128)S(1)} %bitcast.3) | data formatting | bytes 512
  32.6 0.6 %copy.14 = f32[64,64]{1,0:T(8,128)} copy(f32[64,64]{1,0:T(8,128)S(1)} %get-tuple-element.19) | data formatting | bytes 32768

commit v5 on v4

--- a/solution.py
+++ b/solution.py
@@ -28,6 +28,13 @@
 def split(x):
     hi = x.astype(bf16)
     return hi, (x - hi.astype(f32)).astype(bf16)
+
+
+def split3(x):
+    hi = x.astype(bf16)
+    rest = x - hi.astype(f32)
+    mid = rest.astype(bf16)
+    return hi, mid, (rest - mid.astype(f32)).astype(bf16)
 
 
 def iota(shape, dim):
@@ -109,9 +116,15 @@
         )
     here = pl.ds(pl.multiple_of(ti * epochs, epochs), epochs)
     b_hi, b_lo = split(basis[:, here])
-    b_two = jnp.concatenate([b_hi, b_lo], axis=0)
-
-    gram = dot(basis[...], basis[...], NT, highest)
+    b_fixed = jnp.concatenate([
+        jnp.concatenate([b_hi, b_lo], axis=0),
+        jnp.concatenate([b_hi, jnp.zeros_like(b_hi)], axis=0),
+    ], axis=1).T
+
+    g1, g2, g3 = split3(basis[...])
+    three = dot(jnp.concatenate([g1, g2, g3], axis=0), g1, NT)
+    low = (three[rows:2 * rows] + dot(g2, g2, NT) * 0.5) + three[2 * rows:]
+    gram = three[:rows] + (low + low.T)
     eye = (iota((rows, rows), 0) == iota((rows, rows), 1)).astype(f32)
     augmented = jnp.concatenate([gram, eye], axis=1)
     tiles = [augmented[i:i + 8] for i in range(0, rows, 8)]
@@ -171,8 +184,8 @@
     for c in range(chunks):
         load(c).wait()
         f_hi, f_lo = split(slab[c * CHUNK:(c + 1) * CHUNK, :])
-        two = dot(b_two, f_hi, NT)
-        part[:, c * CHUNK:(c + 1) * CHUNK] = (two[rows:] + dot(b_hi, f_lo, NT)) + two[:rows]
+        two = dot(jnp.concatenate([f_hi, f_lo], axis=1), b_fixed, NN).T
+        part[:, c * CHUNK:(c + 1) * CHUNK] = two[rows:] + two[:rows]
         core_copy(c).start()
         for k in range(rows * c // chunks, rows * (c + 1) // chunks, 2):
             eliminate(k)
@@ -183,9 +196,11 @@
     for c in range(max(chunks - LAG, 0), chunks):
         pass_on(c)
     j_hi, j_lo = split(slopes[...])
-    cross = dot(j_lo, j_hi, NT)
-    slope_gram[...] = dot(j_hi, j_hi, NT) + (cross + cross.T)
-    inverse = jnp.concatenate(tiles, axis=0)[:, rows:]
+    two = dot(jnp.concatenate([j_hi, j_lo], axis=0), j_hi, NT)
+    low = two[2 * rows:]
+    slope_gram[...] = two[:2 * rows] + (low + low.T)
+    i1, i2, i3 = split3(jnp.concatenate(tiles, axis=0)[:, rows:])
+    i_six = jnp.concatenate([i3, i2, i1, i2, i1, i1], axis=1)
 
     b_three = jnp.concatenate([b_hi, b_hi, b_lo], axis=0)
     moment = jnp.zeros((rows, epochs), f32)
@@ -196,7 +211,9 @@
         total = from_y[c, 0]
         for y in range(1, n_y):
             total = total + from_y[c, y]
-        modes[:, half(c, core)] = dot(inverse, total, NN, highest)
+        p1, p2, p3 = split3(total)
+        p_six = jnp.concatenate([p1, p2, p3, p1, p2, p1], axis=0)
+        modes[:, half(c, core)] = dot(i_six, p_six, NN)
         modes_copy(c, core).start()
 
     mine = pl.ds(pl.multiple_of(ti * share, share), share)

time: 33.4 us -> 33.1 us (level)
  no operation moved by 1% of the time
where the time goes in v5:
time: 33.1 us; the launch traced here: 33 us
  Pallas kernels  28.4 us (86%)
  local copies, waits for them, and re-layouts  3.93 us (12%)
  between operations  0.64 us (2%)
    pallas_call x1, Pallas kernels, local(): pl.pallas_call(functools.partial(kernel, n_space, n_tm, points * n_space)...  28.4 us
    unnamed x4, local copies, waits for them, and re-layouts  3.93 us

profile of v5, /device:TPU:0, one launch (start us, length us, event | category | flops | bytes accessed | tf_op | source)
XLA Modules:
  0.0 33.0 jit_solution(6881765542961128136)
XLA Ops:
  0.6 28.4 %shard_map.66 = (f32[64,2048]{1,0:T(8,128)S(1)}, f32[2048,512]{1,0:T(8,128)S(1)}, f32[1,64]{1,0:T(1,128)S(1)}, f32[64,64]{1,0:T(8,128)S(1)}) custom-call(f32[2048,512]{1,0:T(8,128)} %frame.1, f32[1,32]{1,0:T(1,128)} %bitcast.4, f32[1,32]{1,0:T(1,128)} %bitcast.5), custom_call_target="tpu_custom_call" | custom-call | tf_op jit(solution)/shard_map/pallas_call | solution.py:345
  29.0 0.8 %copy.11 = f32[64,2048]{1,0:T(8,128)} copy(f32[64,2048]{1,0:T(8,128)S(1)} %get-tuple-element.16) | data formatting | bytes 1048576
  29.8 2.0 %copy.12 = f32[2048,512]{1,0:T(8,128)} copy(f32[2048,512]{1,0:T(8,128)S(1)} %get-tuple-element.17) | data formatting | bytes 8388608
  31.8 0.5 %copy.13 = f32[64]{0:T(128)} copy(f32[64]{0:T(128)S(1)} %bitcast.3) | data formatting | bytes 512
  32.3 0.6 %copy.14 = f32[64,64]{1,0:T(8,128)} copy(f32[64,64]{1,0:T(8,128)S(1)} %get-tuple-element.19) | data formatting | bytes 32768

commit v6 on v5

--- a/solution.py
+++ b/solution.py
@@ -132,16 +132,22 @@
 
     def eliminate(k):
         own, o = k // 8, k % 8
-        r0, r1 = tiles[own][o:o + 1], tiles[own][o + 1:o + 2]
-        a, b = r0[:, k:k + 1], r0[:, k + 1:k + 2]
-        c, d = r1[:, k:k + 1], r1[:, k + 1:k + 2]
+        full = (8, 2 * rows)
+        t = tiles[own]
+        left = jnp.broadcast_to(t[:, k:k + 1], full)
+        right = jnp.broadcast_to(t[:, k + 1:k + 2], full)
+        a, c = (jnp.broadcast_to(left[i:i + 1], full) for i in (o, o + 1))
+        b, d = (jnp.broadcast_to(right[i:i + 1], full) for i in (o, o + 1))
+        r0, r1 = (jnp.broadcast_to(t[i:i + 1], full) for i in (o, o + 1))
         scale = 1.0 / (a * d - b * c)
         p0 = (d * r0 - b * r1) * scale
         p1 = (a * r1 - c * r0) * scale
         for i in range(len(tiles)):
-            t = tiles[i]
-            tiles[i] = t - t[:, k:k + 1] * p0 - t[:, k + 1:k + 2] * p1
-        tiles[own] = jnp.where(row_id == o, p0, jnp.where(row_id == o + 1, p1, tiles[own]))
+            if i != own:
+                u = tiles[i]
+                tiles[i] = u - u[:, k:k + 1] * p0 - u[:, k + 1:k + 2] * p1
+        tiles[own] = jnp.where(
+            row_id == o, p0, jnp.where(row_id == o + 1, p1, t - left * p0 - right * p1))
 
     pl.semaphore_wait(barrier, n_space + n_tm - 2)
 

time: 33.1 us -> 30.8 us (0.931)
  Pallas kernels: 28.4 us -> 26 us
    pallas_call x1, Pallas kernels: 28.4 us -> 26 us  [local(): pl.pallas_call(functools.partial(kernel, n_space, n_tm, points * n_space)...]
where the time goes in v6:
time: 30.8 us; the launch traced here: 30.6 us
  Pallas kernels  26 us (84%)
  local copies, waits for them, and re-layouts  3.93 us (13%)
  between operations  0.64 us (2%)
    pallas_call x1, Pallas kernels, local(): pl.pallas_call(functools.partial(kernel, n_space, n_tm, points * n_space)...  26 us
    unnamed x4, local copies, waits for them, and re-layouts  3.93 us

profile of v6, /device:TPU:0, one launch (start us, length us, event | category | flops | bytes accessed | tf_op | source)
XLA Modules:
  0.0 30.6 jit_solution(11510108951664438174)
XLA Ops:
  0.6 26.0 %shard_map.66 = (f32[64,2048]{1,0:T(8,128)S(1)}, f32[2048,512]{1,0:T(8,128)S(1)}, f32[1,64]{1,0:T(1,128)S(1)}, f32[64,64]{1,0:T(8,128)S(1)}) custom-call(f32[2048,512]{1,0:T(8,128)} %frame.1, f32[1,32]{1,0:T(1,128)} %bitcast.4, f32[1,32]{1,0:T(1,128)} %bitcast.5), custom_call_target="tpu_custom_call" | custom-call | tf_op jit(solution)/shard_map/pallas_call | solution.py:351
  26.7 0.8 %copy.11 = f32[64,2048]{1,0:T(8,128)} copy(f32[64,2048]{1,0:T(8,128)S(1)} %get-tuple-element.16) | data formatting | bytes 1048576
  27.5 2.0 %copy.12 = f32[2048,512]{1,0:T(8,128)} copy(f32[2048,512]{1,0:T(8,128)S(1)} %get-tuple-element.17) | data formatting | bytes 8388608
  29.5 0.5 %copy.13 = f32[64]{0:T(128)} copy(f32[64]{0:T(128)S(1)} %bitcast.3) | data formatting | bytes 512
  30.0 0.6 %copy.14 = f32[64,64]{1,0:T(8,128)} copy(f32[64,64]{1,0:T(8,128)S(1)} %get-tuple-element.19) | data formatting | bytes 32768

commit v7 on v6

--- a/solution.py
+++ b/solution.py
@@ -14,10 +14,10 @@
 NT = (((1,), (1,)), ((), ()))
 TN = (((0,), (0,)), ((), ()))
 MESH = pl.DeviceIdType.MESH
-CHUNK = 256
+CHUNK = 512
 HALF = CHUNK // 2
-AHEAD = 4
-LAG = 2
+AHEAD = 3
+LAG = 1
 BLOCK = 128
 
 

time: 30.8 us -> 31.3 us (1.016)
  Pallas kernels: 26 us -> 26.5 us
    pallas_call x1, Pallas kernels: 26 us -> 26.5 us  [local(): pl.pallas_call(functools.partial(kernel, n_space, n_tm, points * n_space)...]
where the time goes in v7:
time: 31.3 us; the launch traced here: 31.1 us
  Pallas kernels  26.5 us (85%)
  local copies, waits for them, and re-layouts  3.93 us (13%)
  between operations  0.64 us (2%)
    pallas_call x1, Pallas kernels, local(): pl.pallas_call(functools.partial(kernel, n_space, n_tm, points * n_space)...  26.5 us
    unnamed x4, local copies, waits for them, and re-layouts  3.93 us

profile of v7, /device:TPU:0, one launch (start us, length us, event | category | flops | bytes accessed | tf_op | source)
XLA Modules:
  0.0 31.1 jit_solution(10849974309808537805)
XLA Ops:
  0.6 26.5 %shard_map.66 = (f32[64,2048]{1,0:T(8,128)S(1)}, f32[2048,512]{1,0:T(8,128)S(1)}, f32[1,64]{1,0:T(1,128)S(1)}, f32[64,64]{1,0:T(8,128)S(1)}) custom-call(f32[2048,512]{1,0:T(8,128)} %frame.1, f32[1,32]{1,0:T(1,128)} %bitcast.4, f32[1,32]{1,0:T(1,128)} %bitcast.5), custom_call_target="tpu_custom_call" | custom-call | tf_op jit(solution)/shard_map/pallas_call | solution.py:351
  27.2 0.8 %copy.11 = f32[64,2048]{1,0:T(8,128)} copy(f32[64,2048]{1,0:T(8,128)S(1)} %get-tuple-element.16) | data formatting | bytes 1048576
  28.0 2.0 %copy.12 = f32[2048,512]{1,0:T(8,128)} copy(f32[2048,512]{1,0:T(8,128)S(1)} %get-tuple-element.17) | data formatting | bytes 8388608
  30.0 0.5 %copy.13 = f32[64]{0:T(128)} copy(f32[64]{0:T(128)S(1)} %bitcast.3) | data formatting | bytes 512
  30.5 0.6 %copy.14 = f32[64,64]{1,0:T(8,128)} copy(f32[64,64]{1,0:T(8,128)S(1)} %get-tuple-element.19) | data formatting | bytes 32768
